TPU v7x, 32 devices: a whole 2x2x4 slice. The times are simulated.
32 devices in a mesh: lat: 8 (over y, x, core), lon: 4 (over z).
Axes of the slice: x: 2, y: 2, z: 4, core: 2. Of those that a mesh axis runs over, the one named last changes fastest.
Arguments:
- initial: float32 [64, 128, 512], P(None, 'lat', 'lon'), may hold values from -6 to 6
- east_wind: float32 [64, 128, 512], P(None, 'lat', 'lon'), may hold values from -2.5 to 2.5
- north_wind: float32 [64, 128, 512], P(None, 'lat', 'lon'), may hold values from -2.5 to 2.5
- east_mask: int32 [64, 128, 512], P(None, 'lat', 'lon'), may hold values from 0 to 1
- north_mask: int32 [64, 128, 512], P(None, 'lat', 'lon'), may hold values from 0 to 1
- mixing: float32 [63], replicated, may hold values from 0.02 to 0.2
- obs_cell: int32 [8, 4, 4, 256], P('lat', 'lon'), may hold values from 0 to 2047
- obs_level: int32 [8, 4, 4, 256], P('lat', 'lon'), may hold values from 0 to 63
- obs_value: float32 [8, 4, 4, 256], P('lat', 'lon'), may hold values from -6 to 6
- obs_weight: float32 [8, 4, 4, 256], P('lat', 'lon'), may hold values from 0.2 to 2
Outputs:
- gradient: float32 [64, 128, 512], P(None, 'lat', 'lon')
- cost: float32 [], replicated
Inputs may be any that keep to these rules, and one draw needn't show every extreme that they name: `obs_cell`: row times 128 plus column within the block.
All inputs are finite; a program needn't handle non-finite values.
Results may differ from a plain program's by a relative error of at most 0.0003.
Values sent between devices are 32-bit elements; how exact they have to be, the bound alone decides.
A program may use at most 64 MiB of HBM per device.

v0:
```python
import functools

import jax
import jax.numpy as jnp
from jax import lax
from jax.experimental import pallas as pl
from jax.experimental.pallas import tpu as pltpu
from jax.sharding import PartitionSpec as P

STEPS = 4
MESH = pl.DeviceIdType.MESH


def halves(value):
    top = value.astype(jnp.bfloat16)
    return top, (value - top.astype(jnp.float32)).astype(jnp.bfloat16)


def window(
    n_lat, n_lon, levels, rows, cols,
    start_ref, ew_ref, nw_ref, em_ref, nm_ref, mix_ref,
    cell_ref, level_ref, value_ref, weight_ref,
    grad_ref, cost_ref,
    field, source, diag, west_p, west_q, east_p, east_q, south_p, south_q,
    up, down, edge_row, edge_col, packed, face_out, face_in, cost_lon, cost_lat,
    send_sem, recv_sem, face_send, face_recv, lon_send, lon_recv, lat_send, lat_recv,
):
    la, lo = lax.axis_index("lat"), lax.axis_index("lon")
    north = (lax.rem(la + 1, n_lat), lo)
    south = (lax.rem(la + n_lat - 1, n_lat), lo)
    east = (la, lax.rem(lo + 1, n_lon))
    west = (la, lax.rem(lo + n_lon - 1, n_lon))
    lat_others = [(lax.rem(la + d, n_lat), lo) for d in range(1, n_lat)]
    lon_others = [(la, lax.rem(lo + d, n_lon)) for d in range(1, n_lon)]

    barrier = pltpu.get_barrier_semaphore()
    for other in lat_others + lon_others:
        pl.semaphore_signal(barrier, inc=1, device_id=other, device_id_type=MESH)

    lane = lax.broadcasted_iota(jnp.int32, (levels, cols), 1)
    first, last = lane == 0, lane == cols - 1

    def remote(src, dst, send, recv, target):
        return pltpu.make_async_remote_copy(
            src_ref=src, dst_ref=dst, send_sem=send, recv_sem=recv,
            device_id=target, device_id_type=MESH,
        )

    def row_copies(t):
        return (
            remote(field.at[t, 0], edge_row.at[t, 1], send_sem.at[t, 0], recv_sem.at[t, 0], south),
            remote(field.at[t, rows - 1], edge_row.at[t, 0], send_sem.at[t, 1], recv_sem.at[t, 1], north),
        )

    def col_copies(t):
        return (
            remote(packed.at[t], edge_col.at[t, 1], send_sem.at[t, 2], recv_sem.at[t, 2], west),
            remote(packed.at[t], edge_col.at[t, 0], send_sem.at[t, 3], recv_sem.at[t, 3], east),
        )

    face_copies = (
        remote(face_out, face_in, face_send.at[0], face_recv.at[0], west),
        remote(south_p.at[0], south_p.at[rows], face_send.at[1], face_recv.at[1], south),
        remote(south_q.at[0], south_q.at[rows], face_send.at[2], face_recv.at[2], south),
    )

    def pack(total, value, row):
        turned = pltpu.roll(value, 2 * row, 1)
        spot = (lane == 2 * row) | (lane == lax.rem(2 * row + cols - 1, cols))
        return jnp.where(spot, turned, total)

    def strided(ref, row):
        return ref[pl.ds(row, levels, stride=rows), :]

    def parts(wind, mask):
        share = jnp.where(mask == 1, jnp.where(wind > 0, 1.0, 0.0), 0.5)
        return wind * share, wind * (1.0 - share)

    edges = jnp.zeros((levels, cols), jnp.float32)
    faces = jnp.zeros((levels, cols), jnp.float32)
    for row in range(rows):
        value = strided(start_ref, row)
        field[0, row] = value
        edges = pack(edges, value, row)
        p, q = parts(strided(ew_ref, row), strided(em_ref, row))
        west_p[row] = p
        west_q[row] = -q
        faces = jnp.where(lane == 2 * row, pltpu.roll(p, 2 * row, 1), faces)
        faces = jnp.where(lane == 2 * row + 1, pltpu.roll(q, 2 * row + 1, 1), faces)
        p, q = parts(strided(nw_ref, row), strided(nm_ref, row))
        if row == 0:
            p = jnp.where(la > 0, p, 0.0)
            q = jnp.where(la > 0, q, 0.0)
        south_p[row] = p
        south_q[row] = -q
    packed[0] = edges
    face_out[...] = faces

    pl.semaphore_wait(barrier, n_lat + n_lon - 2)
    for copy in face_copies + row_copies(0) + col_copies(0):
        copy.start()

    up[levels - 1 : levels, :] = jnp.zeros((1, cols), jnp.float32)
    down[0:1, :] = jnp.zeros((1, cols), jnp.float32)
    for level in range(levels - 1):
        line = jnp.full((1, cols), mix_ref[level], jnp.float32)
        up[level : level + 1, :] = line
        down[level + 1 : level + 2, :] = line

    for copy in face_copies:
        copy.wait_recv()
    column = 1.0 - up[...] - down[...]
    got = face_in[...]
    for row in range(rows):
        p, q = west_p[row], west_q[row]
        turned_p = pltpu.roll(got, (cols - 2 * row) % cols, 1)
        turned_q = -pltpu.roll(got, (cols - 2 * row - 1) % cols, 1)
        p_next = pltpu.roll(jnp.where(first, turned_p, p), cols - 1, 1)
        q_next = pltpu.roll(jnp.where(first, turned_q, q), cols - 1, 1)
        east_p[row] = p_next
        east_q[row] = q_next
        diag[row] = column - q - p_next - south_q[row] - south_p[row + 1]

    def step(t, out, forward, extra, send):
        for copy in row_copies(t) + col_copies(t):
            copy.wait_recv()
        cw, ce, cs, cn = (
            (west_p, east_q, south_p, south_q) if forward else (west_q, east_p, south_q, south_p)
        )
        edge = jnp.where(lax.rem(lane, 2) == 0, edge_col[t, 1], edge_col[t, 0])

        def one(row, below, above):
            value = field[t, row]
            turned = pltpu.roll(edge, lax.rem(cols - 2 * row, cols), 1)
            at_west = pltpu.roll(jnp.where(last, turned, value), 1, 1)
            at_east = pltpu.roll(jnp.where(first, turned, value), cols - 1, 1)
            higher = pltpu.roll(value, levels - 1, 0)
            lower = pltpu.roll(value, 1, 0)
            new = (
                (diag[row] * value + cw[row] * at_west)
                + (ce[row] * at_east + cs[row] * below)
                + (cn[row + 1] * above + up[...] * higher)
                + down[...] * lower
            )
            if extra is not None:
                new = new + source[extra, pl.ds(row * levels, levels), :]
            return new

        def put(row, new):
            if out is None:
                grad_ref[pl.ds(row, levels, stride=rows), :] = new
            else:
                field[out, row] = new

        low = one(0, edge_row[t, 0], field[t, 1])
        put(0, low)
        high = one(rows - 1, field[t, rows - 2], edge_row[t, 1])
        put(rows - 1, high)
        if send:
            for copy in row_copies(out):
                copy.start()
        total = pack(pack(jnp.zeros_like(low), low, 0), high, rows - 1)

        def inner(i, total):
            for row in (1 + 2 * i, 2 + 2 * i):
                new = one(row, field[t, row - 1], field[t, row + 1])
                put(row, new)
                if send:
                    total = pack(total, new, row)
            return total

        total = lax.fori_loop(0, (rows - 2) // 2, inner, total)
        if send:
            packed[out] = total
            for copy in col_copies(out):
                copy.start()

    def observe(k, slot):
        n_obs = cell_ref.shape[1]
        cell = cell_ref[k : k + 1, :]
        place = (cell // cols) * levels + level_ref[k : k + 1, :]
        col = lax.rem(cell, cols)
        cols_hot = lax.broadcasted_iota(jnp.int32, (cols, n_obs), 0) == col
        pick = jnp.where(cols_hot, 1.0, 0.0).astype(jnp.bfloat16)

        def gather(row, total):
            top, rest = halves(field[slot, row])
            values = jnp.dot(top, pick, preferred_element_type=jnp.float32) + jnp.dot(
                rest, pick, preferred_element_type=jnp.float32
            )
            spots = lax.broadcasted_iota(jnp.int32, (levels, n_obs), 0) + row * levels
            return total + jnp.where(spots == place, values, 0.0)

        found = lax.fori_loop(0, rows, gather, jnp.zeros((levels, n_obs), jnp.float32))
        innovation = jnp.sum(found, axis=0, keepdims=True) - value_ref[k : k + 1, :]
        weighted = weight_ref[k : k + 1, :] * innovation
        top, rest = halves(weighted)
        zero = jnp.zeros((), jnp.float32)
        spread_top = jnp.where(cols_hot, top.astype(jnp.float32), zero).astype(jnp.bfloat16)
        spread_rest = jnp.where(cols_hot, rest.astype(jnp.float32), zero).astype(jnp.bfloat16)

        def scatter(row, _):
            spots = lax.broadcasted_iota(jnp.int32, (levels, n_obs), 0) + row * levels
            hot = jnp.where(spots == place, 1.0, 0.0).astype(jnp.bfloat16)
            dims = (((1,), (1,)), ((), ()))
            value = lax.dot_general(
                hot, spread_top, dims, preferred_element_type=jnp.float32
            ) + lax.dot_general(hot, spread_rest, dims, preferred_element_type=jnp.float32)
            if k == STEPS - 1:
                field[STEPS, row] = value
            else:
                source[k, pl.ds(row * levels, levels), :] = value
            return 0

        lax.fori_loop(0, rows, scatter, 0)
        return 0.5 * jnp.sum(weighted * innovation)

    cost = jnp.zeros((), jnp.float32)
    for k in range(STEPS):
        final = k == STEPS - 1
        slot = 2 * STEPS if final else k + 1
        step(k, slot, True, None, not final)
        cost = cost + observe(k, slot)

    for copy in row_copies(STEPS):
        copy.start()
    total = jnp.zeros((levels, cols), jnp.float32)
    for row in range(rows):
        total = pack(total, field[STEPS, row], row)
    packed[STEPS] = total
    for copy in col_copies(STEPS):
        copy.start()

    def spread(mine, board, others, send, recv):
        return [
            remote(board.at[mine], board.at[mine], send.at[d], recv.at[d], other)
            for d, other in enumerate(others)
        ]

    def drain(board, others, send, recv):
        for d, other in enumerate(others):
            copy = remote(board.at[0], board.at[0], send.at[d], recv.at[d], other)
            copy.wait_send()
            copy.wait_recv()

    cost_lon[lo] = jnp.full((8, 128), cost, jnp.float32)
    for copy in spread(lo, cost_lon, lon_others, lon_send, lon_recv):
        copy.start()

    for k in range(STEPS):
        final = k == STEPS - 1
        slot = STEPS + k
        step(slot, None if final else slot + 1, False, None if final else STEPS - 2 - k, not final)
        if k == 1:
            drain(cost_lon, lon_others, lon_send, lon_recv)
            cost_lat[la] = jnp.sum(cost_lon[...], axis=0)
            for copy in spread(la, cost_lat, lat_others, lat_send, lat_recv):
                copy.start()
    drain(cost_lat, lat_others, lat_send, lat_recv)
    cost_ref[...] = jnp.sum(cost_lat[...], axis=0)

    for copy in face_copies:
        copy.wait_send()
    for t in range(2 * STEPS):
        for copy in row_copies(t) + col_copies(t):
            copy.wait_send()


def on_device(
    n_lat, n_lon,
    initial, east_wind, north_wind, east_mask, north_mask, mixing,
    obs_cell, obs_level, obs_value, obs_weight,
):
    levels, rows, cols = initial.shape
    n_obs = obs_cell.shape[-1]
    flat = (levels * rows, cols)
    f32 = jnp.float32
    vmem = pl.BlockSpec(memory_space=pltpu.VMEM)
    dma = pltpu.SemaphoreType.DMA
    gradient, cost = pl.pallas_call(
        functools.partial(window, n_lat, n_lon, levels, rows, cols),
        out_shape=(jax.ShapeDtypeStruct(flat, f32), jax.ShapeDtypeStruct((8, 128), f32)),
        in_specs=[vmem] * 5 + [pl.BlockSpec(memory_space=pltpu.SMEM)] + [vmem] * 4,
        out_specs=(vmem, vmem),
        scratch_shapes=[
            pltpu.VMEM((2 * STEPS + 1, rows, levels, cols), f32),
            pltpu.VMEM((STEPS - 1,) + flat, f32),
            pltpu.VMEM((rows, levels, cols), f32),
            pltpu.VMEM((rows, levels, cols), f32),
            pltpu.VMEM((rows, levels, cols), f32),
            pltpu.VMEM((rows, levels, cols), f32),
            pltpu.VMEM((rows, levels, cols), f32),
            pltpu.VMEM((rows + 1, levels, cols), f32),
            pltpu.VMEM((rows + 1, levels, cols), f32),
            pltpu.VMEM((levels, cols), f32),
            pltpu.VMEM((levels, cols), f32),
            pltpu.VMEM((2 * STEPS, 2, levels, cols), f32),
            pltpu.VMEM((2 * STEPS, 2, levels, cols), f32),
            pltpu.VMEM((2 * STEPS, levels, cols), f32),
            pltpu.VMEM((levels, cols), f32),
            pltpu.VMEM((levels, cols), f32),
            pltpu.VMEM((n_lon, 8, 128), f32),
            pltpu.VMEM((n_lat, 8, 128), f32),
            dma((2 * STEPS, 4)),
            dma((2 * STEPS, 4)),
            dma((3,)),
            dma((3,)),
            dma((n_lon - 1,)),
            dma((n_lon - 1,)),
            dma((n_lat - 1,)),
            dma((n_lat - 1,)),
        ],
        compiler_params=pltpu.CompilerParams(
            collective_id=0, has_side_effects=True, vmem_limit_bytes=48 * 1024 * 1024
        ),
        cost_estimate=pl.CostEstimate(
            flops=8 * 14 * levels * rows * cols, bytes_accessed=24 * levels * rows * cols, transcendentals=0
        ),
    )(
        initial.reshape(flat), east_wind.reshape(flat), north_wind.reshape(flat),
        east_mask.reshape(flat), north_mask.reshape(flat), mixing,
        obs_cell.reshape(STEPS, n_obs), obs_level.reshape(STEPS, n_obs),
        obs_value.reshape(STEPS, n_obs), obs_weight.reshape(STEPS, n_obs),
    )
    return gradient.reshape(levels, rows, cols), cost[0, 0]


def solution(mesh):
    grid = P(None, "lat", "lon")
    spots = P("lat", "lon", None, None)
    return jax.shard_map(
        functools.partial(on_device, mesh.shape["lat"], mesh.shape["lon"]),
        mesh=mesh,
        in_specs=(grid,) * 5 + (P(),) + (spots,) * 4,
        out_specs=(grid, P()),
        check_vma=False,
    )
```

profile of v0, /device:TPU:0, one launch (start us, length us, event | category | flops | bytes accessed | tf_op | source)
XLA Modules:
  0.0 72.2 jit_solution(15343683262301765898)
XLA Ops:
  0.6 0.0 copy-start.8
  0.6 0.0 copy-start.7
  0.7 0.0 copy-start.6
  0.7 0.0 copy-start.5
  0.7 0.0 copy-start.9
  0.7 0.6 copy-done.8
  1.3 0.0 copy-done.7
  1.3 0.0 copy-done.6
  1.4 0.0 copy-done.5
  1.4 0.0 copy-done.9
  1.4 0.0 copy-start
  1.4 1.0 %copy-done = f32[64,16,128]{2,1,0:T(8,128)S(1)} copy-done((f32[64,16,128]{2,1,0:T(8,128)S(1)}, f32[64,16,128]{2,1,0:T(8,128)}, u32[]{:S(2)}) %copy-start) | copy-done | bytes 524312
  2.4 0.0 copy-start.1
  2.4 1.0 %copy-done.1 = f32[64,16,128]{2,1,0:T(8,128)S(1)} copy-done((f32[64,16,128]{2,1,0:T(8,128)S(1)}, f32[64,16,128]{2,1,0:T(8,128)}, u32[]{:S(2)}) %copy-start.1) | copy-done | bytes 524312
  3.5 0.0 copy-start.2
  3.5 1.0 %copy-done.2 = f32[64,16,128]{2,1,0:T(8,128)S(1)} copy-done((f32[64,16,128]{2,1,0:T(8,128)S(1)}, f32[64,16,128]{2,1,0:T(8,128)}, u32[]{:S(2)}) %copy-start.2) | copy-done | bytes 524312
  4.5 0.0 copy-start.3
  4.5 1.0 %copy-done.3 = s32[64,16,128]{2,1,0:T(8,128)S(1)} copy-done((s32[64,16,128]{2,1,0:T(8,128)S(1)}, s32[64,16,128]{2,1,0:T(8,128)}, u32[]{:S(2)}) %copy-start.3) | copy-done | bytes 524312
  5.5 0.0 copy-start.4
  5.5 1.0 %copy-done.4 = s32[64,16,128]{2,1,0:T(8,128)S(1)} copy-done((s32[64,16,128]{2,1,0:T(8,128)S(1)}, s32[64,16,128]{2,1,0:T(8,128)}, u32[]{:S(2)}) %copy-start.4) | copy-done | bytes 524312
  6.6 64.3 %shard_map.113 = (f32[1024,128]{1,0:T(8,128)S(1)}, f32[8,128]{1,0:T(8,128)S(1)}) custom-call(f32[1024,128]{1,0:T(8,128)S(1)} %bitcast.12, f32[1024,128]{1,0:T(8,128)S(1)} %bitcast.13, f32[1024,128]{1,0:T(8,128)S(1)} %bitcast.14, s32[1024,128]{1,0:T(8,128)S(1)} %bitcast.15, s32[1024,128]{1,0:T(8,128)S(1)} %bitcast.16, f32[63]{0:T(128)S(1)} %copy-done.9, ...), custom_call_target="tpu_custom_call" | custom-call | flops 14680064 | bytes 3145728 | tf_op jit(solution)/shard_map/pallas_call | solution.py:280
  70.9 0.5 slice.3
  71.4 0.8 %copy.13 = f32[64,16,128]{2,1,0:T(8,128)} copy(f32[64,16,128]{2,1,0:T(8,128)S(1)} %bitcast.11) | data formatting | bytes 1048576
Async XLA Ops:
  0.6 0.7 copy-start.8
  0.6 0.7 copy-start.7
  0.7 0.7 copy-start.6
  0.7 0.7 copy-start.5
  0.7 0.7 copy-start.9
  1.4 1.0 %copy-start = (f32[64,16,128]{2,1,0:T(8,128)S(1)}, f32[64,16,128]{2,1,0:T(8,128)}, u32[]{:S(2)}) copy-start(f32[64,16,128]{2,1,0:T(8,128)} %param.10) | copy-start | bytes 1572868
  2.4 1.0 %copy-start.1 = (f32[64,16,128]{2,1,0:T(8,128)S(1)}, f32[64,16,128]{2,1,0:T(8,128)}, u32[]{:S(2)}) copy-start(f32[64,16,128]{2,1,0:T(8,128)} %param.11) | copy-start | bytes 1572868
  3.5 1.0 %copy-start.2 = (f32[64,16,128]{2,1,0:T(8,128)S(1)}, f32[64,16,128]{2,1,0:T(8,128)}, u32[]{:S(2)}) copy-start(f32[64,16,128]{2,1,0:T(8,128)} %param.12) | copy-start | bytes 1572868
  4.5 1.0 %copy-start.3 = (s32[64,16,128]{2,1,0:T(8,128)S(1)}, s32[64,16,128]{2,1,0:T(8,128)}, u32[]{:S(2)}) copy-start(s32[64,16,128]{2,1,0:T(8,128)} %param.13) | copy-start | bytes 1572868
  5.5 1.0 %copy-start.4 = (s32[64,16,128]{2,1,0:T(8,128)S(1)}, s32[64,16,128]{2,1,0:T(8,128)}, u32[]{:S(2)}) copy-start(s32[64,16,128]{2,1,0:T(8,128)} %param.14) | copy-start | bytes 1572868
where the time goes:
time: 72.6 us; the launch traced here: 72.2 us
  Pallas kernels  64.3 us (89%)
  local copies, waits for them, and re-layouts  7.21 us (10%)
    pallas_call x1, Pallas kernels, on_device(): pl.pallas_call(functools.partial(window, n_lat, n_lon, levels, rows, cols...  64.3 us
    unnamed x21, local copies, waits for them, and re-layouts  6.7 us

commit v1 on v0

--- a/solution.py
+++ b/solution.py
@@ -18,13 +18,16 @@
 
 def window(
     n_lat, n_lon, levels, rows, cols,
-    start_ref, ew_ref, nw_ref, em_ref, nm_ref, mix_ref,
-    cell_ref, level_ref, value_ref, weight_ref,
-    grad_ref, cost_ref,
-    field, source, diag, west_p, west_q, east_p, east_q, south_p, south_q,
-    up, down, edge_row, edge_col, packed, face_out, face_in, cost_lon, cost_lat,
-    send_sem, recv_sem, face_send, face_recv, lon_send, lon_recv, lat_send, lat_recv,
+    *refs,
 ):
+    sources, (grad_ref, cost_ref), landed, rest = refs[:10], refs[10:12], refs[12:22], refs[22:]
+    start_ref, ew_ref, nw_ref, em_ref, nm_ref, mix_ref = landed[:6]
+    cell_ref, level_ref, value_ref, weight_ref = landed[6:]
+    (
+        field, source, diag, west_p, west_q, east_p, east_q, south_p, south_q,
+        up, down, edge_row, edge_col, packed, face_out, face_in, cost_lon, cost_lat,
+        send_sem, recv_sem, face_send, face_recv, lon_send, lon_recv, lat_send, lat_recv, load_sem,
+    ) = rest
     la, lo = lax.axis_index("lat"), lax.axis_index("lon")
     north = (lax.rem(la + 1, n_lat), lo)
     south = (lax.rem(la + n_lat - 1, n_lat), lo)
@@ -33,6 +36,12 @@
     lat_others = [(lax.rem(la + d, n_lat), lo) for d in range(1, n_lat)]
     lon_others = [(la, lax.rem(lo + d, n_lon)) for d in range(1, n_lon)]
 
+    loads = [
+        pltpu.make_async_copy(src, dst, load_sem.at[i])
+        for i, (src, dst) in enumerate(zip(sources, landed))
+    ]
+    for load in loads:
+        load.start()
     barrier = pltpu.get_barrier_semaphore()
     for other in lat_others + lon_others:
         pl.semaphore_signal(barrier, inc=1, device_id=other, device_id_type=MESH)
@@ -66,7 +75,7 @@
 
     def pack(total, value, row):
         turned = pltpu.roll(value, 2 * row, 1)
-        spot = (lane == 2 * row) | (lane == lax.rem(2 * row + cols - 1, cols))
+        spot = (lane == 2 * row) | (lane == (2 * row + cols - 1) % cols)
         return jnp.where(spot, turned, total)
 
     def strided(ref, row):
@@ -76,6 +85,8 @@
         share = jnp.where(mask == 1, jnp.where(wind > 0, 1.0, 0.0), 0.5)
         return wind * share, wind * (1.0 - share)
 
+    for load in loads[:5]:
+        load.wait()
     edges = jnp.zeros((levels, cols), jnp.float32)
     faces = jnp.zeros((levels, cols), jnp.float32)
     for row in range(rows):
@@ -100,6 +111,8 @@
     for copy in face_copies + row_copies(0) + col_copies(0):
         copy.start()
 
+    for load in loads[5:]:
+        load.wait()
     up[levels - 1 : levels, :] = jnp.zeros((1, cols), jnp.float32)
     down[0:1, :] = jnp.zeros((1, cols), jnp.float32)
     for level in range(levels - 1):
@@ -131,7 +144,7 @@
 
         def one(row, below, above):
             value = field[t, row]
-            turned = pltpu.roll(edge, lax.rem(cols - 2 * row, cols), 1)
+            turned = pltpu.roll(edge, (cols - 2 * row) % cols, 1)
             at_west = pltpu.roll(jnp.where(last, turned, value), 1, 1)
             at_east = pltpu.roll(jnp.where(first, turned, value), cols - 1, 1)
             higher = pltpu.roll(value, levels - 1, 0)
@@ -143,7 +156,7 @@
                 + down[...] * lower
             )
             if extra is not None:
-                new = new + source[extra, pl.ds(row * levels, levels), :]
+                new = new + source[extra, row * levels : (row + 1) * levels, :]
             return new
 
         def put(row, new):
@@ -161,15 +174,11 @@
                 copy.start()
         total = pack(pack(jnp.zeros_like(low), low, 0), high, rows - 1)
 
-        def inner(i, total):
-            for row in (1 + 2 * i, 2 + 2 * i):
-                new = one(row, field[t, row - 1], field[t, row + 1])
-                put(row, new)
-                if send:
-                    total = pack(total, new, row)
-            return total
-
-        total = lax.fori_loop(0, (rows - 2) // 2, inner, total)
+        for row in range(1, rows - 1):
+            new = one(row, field[t, row - 1], field[t, row + 1])
+            put(row, new)
+            if send:
+                total = pack(total, new, row)
         if send:
             packed[out] = total
             for copy in col_copies(out):
@@ -182,37 +191,32 @@
         col = lax.rem(cell, cols)
         cols_hot = lax.broadcasted_iota(jnp.int32, (cols, n_obs), 0) == col
         pick = jnp.where(cols_hot, 1.0, 0.0).astype(jnp.bfloat16)
-
-        def gather(row, total):
-            top, rest = halves(field[slot, row])
-            values = jnp.dot(top, pick, preferred_element_type=jnp.float32) + jnp.dot(
-                rest, pick, preferred_element_type=jnp.float32
+        pick = jnp.concatenate([pick, pick], 0)
+        group = 4 * levels
+        spots = lax.broadcasted_iota(jnp.int32, (group, n_obs), 0)
+
+        found = jnp.zeros((8, n_obs), jnp.float32)
+        for row in range(0, rows, 4):
+            value = field[slot, row : row + 4].reshape(group, cols)
+            values = jnp.dot(
+                jnp.concatenate(halves(value), 1), pick, preferred_element_type=jnp.float32
             )
-            spots = lax.broadcasted_iota(jnp.int32, (levels, n_obs), 0) + row * levels
-            return total + jnp.where(spots == place, values, 0.0)
-
-        found = lax.fori_loop(0, rows, gather, jnp.zeros((levels, n_obs), jnp.float32))
+            values = jnp.where(spots == place - row * levels, values, 0.0)
+            found = found + jnp.sum(values.reshape(group // 8, 8, n_obs), axis=0)
         innovation = jnp.sum(found, axis=0, keepdims=True) - value_ref[k : k + 1, :]
         weighted = weight_ref[k : k + 1, :] * innovation
-        top, rest = halves(weighted)
-        zero = jnp.zeros((), jnp.float32)
-        spread_top = jnp.where(cols_hot, top.astype(jnp.float32), zero).astype(jnp.bfloat16)
-        spread_rest = jnp.where(cols_hot, rest.astype(jnp.float32), zero).astype(jnp.bfloat16)
-
-        def scatter(row, _):
-            spots = lax.broadcasted_iota(jnp.int32, (levels, n_obs), 0) + row * levels
-            hot = jnp.where(spots == place, 1.0, 0.0).astype(jnp.bfloat16)
-            dims = (((1,), (1,)), ((), ()))
-            value = lax.dot_general(
-                hot, spread_top, dims, preferred_element_type=jnp.float32
-            ) + lax.dot_general(hot, spread_rest, dims, preferred_element_type=jnp.float32)
+        share = jnp.concatenate(halves(jnp.where(cols_hot, weighted, 0.0)), 0)
+
+        for row in range(0, rows, 4):
+            hot = jnp.where(spots == place - row * levels, 1.0, 0.0).astype(jnp.bfloat16)
+            both = lax.dot_general(
+                hot, share, (((1,), (1,)), ((), ())), preferred_element_type=jnp.float32
+            )
+            value = both[:, :cols] + both[:, cols:]
             if k == STEPS - 1:
-                field[STEPS, row] = value
+                field[STEPS, row : row + 4] = value.reshape(4, levels, cols)
             else:
-                source[k, pl.ds(row * levels, levels), :] = value
-            return 0
-
-        lax.fori_loop(0, rows, scatter, 0)
+                source[k, row * levels : row * levels + group, :] = value
         return 0.5 * jnp.sum(weighted * innovation)
 
     cost = jnp.zeros((), jnp.float32)
@@ -257,7 +261,7 @@
             for copy in spread(la, cost_lat, lat_others, lat_send, lat_recv):
                 copy.start()
     drain(cost_lat, lat_others, lat_send, lat_recv)
-    cost_ref[...] = jnp.sum(cost_lat[...], axis=0)
+    cost_ref[0, 0] = jnp.sum(cost_lat[...], axis=0)[0, 0]
 
     for copy in face_copies:
         copy.wait_send()
@@ -279,10 +283,20 @@
     dma = pltpu.SemaphoreType.DMA
     gradient, cost = pl.pallas_call(
         functools.partial(window, n_lat, n_lon, levels, rows, cols),
-        out_shape=(jax.ShapeDtypeStruct(flat, f32), jax.ShapeDtypeStruct((8, 128), f32)),
-        in_specs=[vmem] * 5 + [pl.BlockSpec(memory_space=pltpu.SMEM)] + [vmem] * 4,
-        out_specs=(vmem, vmem),
+        out_shape=(jax.ShapeDtypeStruct(flat, f32), jax.ShapeDtypeStruct((1, 1), f32)),
+        in_specs=[pl.BlockSpec(memory_space=pl.ANY)] * 10,
+        out_specs=(vmem, pl.BlockSpec(memory_space=pltpu.SMEM)),
         scratch_shapes=[
+            pltpu.VMEM(flat, f32),
+            pltpu.VMEM(flat, f32),
+            pltpu.VMEM(flat, f32),
+            pltpu.VMEM(flat, jnp.int32),
+            pltpu.VMEM(flat, jnp.int32),
+            pltpu.SMEM(mixing.shape, f32),
+            pltpu.VMEM((STEPS, n_obs), jnp.int32),
+            pltpu.VMEM((STEPS, n_obs), jnp.int32),
+            pltpu.VMEM((STEPS, n_obs), f32),
+            pltpu.VMEM((STEPS, n_obs), f32),
             pltpu.VMEM((2 * STEPS + 1, rows, levels, cols), f32),
             pltpu.VMEM((STEPS - 1,) + flat, f32),
             pltpu.VMEM((rows, levels, cols), f32),
@@ -309,6 +323,7 @@
             dma((n_lon - 1,)),
             dma((n_lat - 1,)),
             dma((n_lat - 1,)),
+            dma((10,)),
         ],
         compiler_params=pltpu.CompilerParams(
             collective_id=0, has_side_effects=True, vmem_limit_bytes=48 * 1024 * 1024

time: 72.6 us -> 58.8 us (0.81)
  Pallas kernels: 64.3 us -> 49.3 us
  between operations: 0.69 us -> 2.45 us
    pallas_call x1, Pallas kernels: 64.3 us -> 49.3 us  [on_device(): pl.pallas_call(functools.partial(window, n_lat, n_lon, levels, rows, cols...]
where the time goes in v1:
time: 58.8 us; the launch traced here: 58.4 us
  Pallas kernels  49.3 us (84%)
  local copies, waits for them, and re-layouts  6.7 us (11%)
  between operations  2.45 us (4%)
    pallas_call x1, Pallas kernels, on_device(): pl.pallas_call(functools.partial(window, n_lat, n_lon, levels, rows, cols...  49.3 us
    unnamed x21, local copies, waits for them, and re-layouts  6.7 us

profile of v1, /device:TPU:0, one launch (start us, length us, event | category | flops | bytes accessed | tf_op | source)
XLA Modules:
  0.0 58.4 jit_solution(7931931247112491529)
XLA Ops:
  0.6 0.0 copy-start.8
  0.6 0.0 copy-start.7
  0.7 0.0 copy-start.6
  0.7 0.0 copy-start.5
  0.7 0.0 copy-start.9
  0.7 0.6 %copy-done.8 = f32[1,1,4,256]{3,2,1,0:T(4,128)S(1)} copy-done((f32[1,1,4,256]{3,2,1,0:T(4,128)S(1)}, f32[1,1,4,256]{3,2,1,0:T(4,128)}, u32[]{:S(2)}) %copy-start.8) | copy-done | bytes 4120
  1.3 0.0 copy-done.7
  1.3 0.0 copy-done.6
  1.4 0.0 copy-done.5
  1.4 0.0 copy-done.9
  1.4 0.0 copy-start
  1.4 1.0 %copy-done = f32[64,16,128]{2,1,0:T(8,128)S(1)} copy-done((f32[64,16,128]{2,1,0:T(8,128)S(1)}, f32[64,16,128]{2,1,0:T(8,128)}, u32[]{:S(2)}) %copy-start) | copy-done | bytes 524312
  2.4 0.0 copy-start.1
  2.4 1.0 %copy-done.1 = f32[64,16,128]{2,1,0:T(8,128)S(1)} copy-done((f32[64,16,128]{2,1,0:T(8,128)S(1)}, f32[64,16,128]{2,1,0:T(8,128)}, u32[]{:S(2)}) %copy-start.1) | copy-done | bytes 524312
  3.5 0.0 copy-start.2
  3.5 1.0 %copy-done.2 = f32[64,16,128]{2,1,0:T(8,128)S(1)} copy-done((f32[64,16,128]{2,1,0:T(8,128)S(1)}, f32[64,16,128]{2,1,0:T(8,128)}, u32[]{:S(2)}) %copy-start.2) | copy-done | bytes 524312
  4.5 0.0 copy-start.3
  4.5 1.0 %copy-done.3 = s32[64,16,128]{2,1,0:T(8,128)S(1)} copy-done((s32[64,16,128]{2,1,0:T(8,128)S(1)}, s32[64,16,128]{2,1,0:T(8,128)}, u32[]{:S(2)}) %copy-start.3) | copy-done | bytes 524312
  5.5 0.0 copy-start.4
  5.5 1.0 %copy-done.4 = s32[64,16,128]{2,1,0:T(8,128)S(1)} copy-done((s32[64,16,128]{2,1,0:T(8,128)S(1)}, s32[64,16,128]{2,1,0:T(8,128)}, u32[]{:S(2)}) %copy-start.4) | copy-done | bytes 524312
  6.6 49.3 %shard_map.113 = (f32[1024,128]{1,0:T(8,128)S(1)}, f32[1,1]{1,0:T(1,128)}) custom-call(f32[1024,128]{1,0:T(8,128)S(1)} %bitcast.12, f32[1024,128]{1,0:T(8,128)S(1)} %bitcast.13, f32[1024,128]{1,0:T(8,128)S(1)} %bitcast.14, s32[1024,128]{1,0:T(8,128)S(1)} %bitcast.15, s32[1024,128]{1,0:T(8,128)S(1)} %bitcast.16, f32[63]{0:T(128)S(1)} %copy-done.9, ...), custom_call_target="tpu_custom_call" | custom-call | flops 14680064 | bytes 3145728 | tf_op jit(solution)/shard_map/pallas_call | solution.py:284
  55.9 0.8 %copy.14 = f32[64,16,128]{2,1,0:T(8,128)} copy(f32[64,16,128]{2,1,0:T(8,128)S(1)} %bitcast.11) | data formatting | bytes 1048576
Async XLA Ops:
  0.6 0.7 %copy-start.8 = (f32[1,1,4,256]{3,2,1,0:T(4,128)S(1)}, f32[1,1,4,256]{3,2,1,0:T(4,128)}, u32[]{:S(2)}) copy-start(f32[1,1,4,256]{3,2,1,0:T(4,128)} %param.19) | copy-start | bytes 12292
  0.6 0.7 %copy-start.7 = (f32[1,1,4,256]{3,2,1,0:T(4,128)S(1)}, f32[1,1,4,256]{3,2,1,0:T(4,128)}, u32[]{:S(2)}) copy-start(f32[1,1,4,256]{3,2,1,0:T(4,128)} %param.18) | copy-start | bytes 12292
  0.7 0.7 %copy-start.6 = (s32[1,1,4,256]{3,2,1,0:T(4,128)S(1)}, s32[1,1,4,256]{3,2,1,0:T(4,128)}, u32[]{:S(2)}) copy-start(s32[1,1,4,256]{3,2,1,0:T(4,128)} %param.17) | copy-start | bytes 12292
  0.7 0.7 %copy-start.5 = (s32[1,1,4,256]{3,2,1,0:T(4,128)S(1)}, s32[1,1,4,256]{3,2,1,0:T(4,128)}, u32[]{:S(2)}) copy-start(s32[1,1,4,256]{3,2,1,0:T(4,128)} %param.16) | copy-start | bytes 12292
  0.7 0.7 %copy-start.9 = (f32[63]{0:T(128)S(1)}, f32[63]{0:T(128)}, u32[]{:S(2)}) copy-start(f32[63]{0:T(128)} %refs_5_.1) | copy-start | bytes 760
  1.4 1.0 %copy-start = (f32[64,16,128]{2,1,0:T(8,128)S(1)}, f32[64,16,128]{2,1,0:T(8,128)}, u32[]{:S(2)}) copy-start(f32[64,16,128]{2,1,0:T(8,128)} %param.10) | copy-start | bytes 1572868
  2.4 1.0 %copy-start.1 = (f32[64,16,128]{2,1,0:T(8,128)S(1)}, f32[64,16,128]{2,1,0:T(8,128)}, u32[]{:S(2)}) copy-start(f32[64,16,128]{2,1,0:T(8,128)} %param.11) | copy-start | bytes 1572868
  3.5 1.0 %copy-start.2 = (f32[64,16,128]{2,1,0:T(8,128)S(1)}, f32[64,16,128]{2,1,0:T(8,128)}, u32[]{:S(2)}) copy-start(f32[64,16,128]{2,1,0:T(8,128)} %param.12) | copy-start | bytes 1572868
  4.5 1.0 %copy-start.3 = (s32[64,16,128]{2,1,0:T(8,128)S(1)}, s32[64,16,128]{2,1,0:T(8,128)}, u32[]{:S(2)}) copy-start(s32[64,16,128]{2,1,0:T(8,128)} %param.13) | copy-start | bytes 1572868
  5.5 1.0 %copy-start.4 = (s32[64,16,128]{2,1,0:T(8,128)S(1)}, s32[64,16,128]{2,1,0:T(8,128)}, u32[]{:S(2)}) copy-start(s32[64,16,128]{2,1,0:T(8,128)} %param.14) | copy-start | bytes 1572868

commit v2 on v1

--- a/solution.py
+++ b/solution.py
@@ -46,8 +46,13 @@
     for other in lat_others + lon_others:
         pl.semaphore_signal(barrier, inc=1, device_id=other, device_id_type=MESH)
 
+    groups = cols // (2 * rows)
+    fold = levels // groups
     lane = lax.broadcasted_iota(jnp.int32, (levels, cols), 1)
     first, last = lane == 0, lane == cols - 1
+    rim = first | last
+    thin = lax.broadcasted_iota(jnp.int32, (fold, cols), 1)
+    even = lax.rem(thin, 2) == 0
 
     def remote(src, dst, send, recv, target):
         return pltpu.make_async_remote_copy(
@@ -74,9 +79,21 @@
     )
 
     def pack(total, value, row):
-        turned = pltpu.roll(value, 2 * row, 1)
-        spot = (lane == 2 * row) | (lane == (2 * row + cols - 1) % cols)
-        return jnp.where(spot, turned, total)
+        for group in range(groups):
+            shift = 2 * row + 2 * rows * group
+            turned = pltpu.roll(value[group * fold : (group + 1) * fold], shift, 1)
+            spot = (thin == shift) | (thin == (shift + cols - 1) % cols)
+            total = jnp.where(spot, turned, total)
+        return total
+
+    def unpack(total, row, more=0):
+        return jnp.concatenate(
+            [
+                pltpu.roll(total, (2 * cols - 2 * row - 2 * rows * group - more) % cols, 1)
+                for group in range(groups)
+            ],
+            0,
+        )
 
     def strided(ref, row):
         return ref[pl.ds(row, levels, stride=rows), :]
@@ -85,30 +102,42 @@
         share = jnp.where(mask == 1, jnp.where(wind > 0, 1.0, 0.0), 0.5)
         return wind * share, wind * (1.0 - share)
 
-    for load in loads[:5]:
-        load.wait()
-    edges = jnp.zeros((levels, cols), jnp.float32)
-    faces = jnp.zeros((levels, cols), jnp.float32)
+    loads[0].wait()
+    edges = jnp.zeros((fold, cols), jnp.float32)
     for row in range(rows):
         value = strided(start_ref, row)
         field[0, row] = value
         edges = pack(edges, value, row)
-        p, q = parts(strided(ew_ref, row), strided(em_ref, row))
-        west_p[row] = p
-        west_q[row] = -q
-        faces = jnp.where(lane == 2 * row, pltpu.roll(p, 2 * row, 1), faces)
-        faces = jnp.where(lane == 2 * row + 1, pltpu.roll(q, 2 * row + 1, 1), faces)
+    packed[0] = edges
+    pl.semaphore_wait(barrier, n_lat + n_lon - 2)
+    for copy in row_copies(0) + col_copies(0):
+        copy.start()
+
+    for load in loads[1:5]:
+        load.wait()
+    faces = jnp.zeros((fold, cols), jnp.float32)
+    for row in range(rows):
         p, q = parts(strided(nw_ref, row), strided(nm_ref, row))
         if row == 0:
             p = jnp.where(la > 0, p, 0.0)
             q = jnp.where(la > 0, q, 0.0)
         south_p[row] = p
         south_q[row] = -q
-    packed[0] = edges
+        own = 1.0 + q
+        p, q = parts(strided(ew_ref, row), strided(em_ref, row))
+        west_p[row] = jnp.where(first, 0.0, p)
+        west_q[row] = jnp.where(first, 0.0, -q)
+        p_next = jnp.where(last, 0.0, pltpu.roll(p, cols - 1, 1))
+        east_p[row] = p_next
+        east_q[row] = jnp.where(last, 0.0, -pltpu.roll(q, cols - 1, 1))
+        diag[row] = own + q - p_next
+        for group in range(groups):
+            shift = 2 * row + 2 * rows * group
+            part = slice(group * fold, (group + 1) * fold)
+            faces = jnp.where(thin == shift, pltpu.roll(p[part], shift, 1), faces)
+            faces = jnp.where(thin == shift + 1, pltpu.roll(q[part], shift + 1, 1), faces)
     face_out[...] = faces
-
-    pl.semaphore_wait(barrier, n_lat + n_lon - 2)
-    for copy in face_copies + row_copies(0) + col_copies(0):
+    for copy in face_copies:
         copy.start()
 
     for load in loads[5:]:
@@ -122,67 +151,69 @@
 
     for copy in face_copies:
         copy.wait_recv()
-    column = 1.0 - up[...] - down[...]
+    column = up[...] + down[...]
     got = face_in[...]
     for row in range(rows):
-        p, q = west_p[row], west_q[row]
-        turned_p = pltpu.roll(got, (cols - 2 * row) % cols, 1)
-        turned_q = -pltpu.roll(got, (cols - 2 * row - 1) % cols, 1)
-        p_next = pltpu.roll(jnp.where(first, turned_p, p), cols - 1, 1)
-        q_next = pltpu.roll(jnp.where(first, turned_q, q), cols - 1, 1)
-        east_p[row] = p_next
-        east_q[row] = q_next
-        diag[row] = column - q - p_next - south_q[row] - south_p[row + 1]
-
-    def step(t, out, forward, extra, send):
+        p_next = jnp.where(last, unpack(got, row, 1), 0.0)
+        diag[row] = diag[row] - column - p_next - south_p[row + 1]
+    rim_ahead = jnp.where(even, faces, -pltpu.roll(got, cols - 2, 1))
+    rim_back = jnp.where(even, -pltpu.roll(faces, cols - 1, 1), pltpu.roll(got, cols - 1, 1))
+
+    def coefs(forward):
+        if forward:
+            return west_p, east_q, south_p, south_q
+        return west_q, east_p, south_q, south_p
+
+    def put(out, row, new):
+        if out is None:
+            grad_ref[pl.ds(row, levels, stride=rows), :] = new
+        else:
+            field[out, row] = new
+
+    def get(out, row):
+        if out is None:
+            return grad_ref[pl.ds(row, levels, stride=rows), :]
+        return field[out, row]
+
+    def inside(t, out, forward, extra, send):
+        cw, ce, cs, cn = coefs(forward)
+        total = jnp.zeros((fold, cols), jnp.float32)
+        for row in range(rows):
+            value = field[t, row]
+            new = (
+                (diag[row] * value + cw[row] * pltpu.roll(value, 1, 1))
+                + (ce[row] * pltpu.roll(value, cols - 1, 1) + up[...] * pltpu.roll(value, levels - 1, 0))
+                + down[...] * pltpu.roll(value, 1, 0)
+            )
+            if row > 0:
+                new = new + cs[row] * field[t, row - 1]
+            if row < rows - 1:
+                new = new + cn[row + 1] * field[t, row + 1]
+            if extra is not None:
+                new = new + source[extra, row * levels : (row + 1) * levels, :]
+            put(out, row, new)
+            if send and 0 < row < rows - 1:
+                total = pack(total, new, row)
+        return total
+
+    def finish(t, out, forward, total, send):
+        cw, ce, cs, cn = coefs(forward)
         for copy in row_copies(t) + col_copies(t):
             copy.wait_recv()
-        cw, ce, cs, cn = (
-            (west_p, east_q, south_p, south_q) if forward else (west_q, east_p, south_q, south_p)
-        )
-        edge = jnp.where(lax.rem(lane, 2) == 0, edge_col[t, 1], edge_col[t, 0])
-
-        def one(row, below, above):
-            value = field[t, row]
-            turned = pltpu.roll(edge, (cols - 2 * row) % cols, 1)
-            at_west = pltpu.roll(jnp.where(last, turned, value), 1, 1)
-            at_east = pltpu.roll(jnp.where(first, turned, value), cols - 1, 1)
-            higher = pltpu.roll(value, levels - 1, 0)
-            lower = pltpu.roll(value, 1, 0)
-            new = (
-                (diag[row] * value + cw[row] * at_west)
-                + (ce[row] * at_east + cs[row] * below)
-                + (cn[row + 1] * above + up[...] * higher)
-                + down[...] * lower
-            )
-            if extra is not None:
-                new = new + source[extra, row * levels : (row + 1) * levels, :]
-            return new
-
-        def put(row, new):
-            if out is None:
-                grad_ref[pl.ds(row, levels, stride=rows), :] = new
-            else:
-                field[out, row] = new
-
-        low = one(0, edge_row[t, 0], field[t, 1])
-        put(0, low)
-        high = one(rows - 1, field[t, rows - 2], edge_row[t, 1])
-        put(rows - 1, high)
+        met = jnp.where(
+            even, pltpu.roll(edge_col[t, 0], 1, 1), pltpu.roll(edge_col[t, 1], cols - 1, 1)
+        )
+        gain = (rim_ahead if forward else rim_back) * met
+        low = get(out, 0) + cs[0] * edge_row[t, 0]
+        high = get(out, rows - 1) + cn[rows] * edge_row[t, 1]
+        put(out, 0, low + jnp.where(rim, unpack(gain, 0), 0.0))
+        put(out, rows - 1, high + jnp.where(rim, unpack(gain, rows - 1), 0.0))
         if send:
-            for copy in row_copies(out):
+            packed[out] = pack(pack(total, low, 0), high, rows - 1) + gain
+            for copy in col_copies(out) + row_copies(out):
                 copy.start()
-        total = pack(pack(jnp.zeros_like(low), low, 0), high, rows - 1)
-
         for row in range(1, rows - 1):
-            new = one(row, field[t, row - 1], field[t, row + 1])
-            put(row, new)
-            if send:
-                total = pack(total, new, row)
-        if send:
-            packed[out] = total
-            for copy in col_copies(out):
-                copy.start()
+            put(out, row, get(out, row) + jnp.where(rim, unpack(gain, row), 0.0))
 
     def observe(k, slot):
         n_obs = cell_ref.shape[1]
@@ -220,15 +251,19 @@
         return 0.5 * jnp.sum(weighted * innovation)
 
     cost = jnp.zeros((), jnp.float32)
+    total = inside(0, 1, True, None, True)
     for k in range(STEPS):
         final = k == STEPS - 1
         slot = 2 * STEPS if final else k + 1
-        step(k, slot, True, None, not final)
+        finish(k, slot, True, total, not final)
+        if not final:
+            ahead = k + 1 == STEPS - 1
+            total = inside(k + 1, 2 * STEPS if ahead else k + 2, True, None, not ahead)
         cost = cost + observe(k, slot)
 
     for copy in row_copies(STEPS):
         copy.start()
-    total = jnp.zeros((levels, cols), jnp.float32)
+    total = jnp.zeros((fold, cols), jnp.float32)
     for row in range(rows):
         total = pack(total, field[STEPS, row], row)
     packed[STEPS] = total
@@ -254,7 +289,9 @@
     for k in range(STEPS):
         final = k == STEPS - 1
         slot = STEPS + k
-        step(slot, None if final else slot + 1, False, None if final else STEPS - 2 - k, not final)
+        out = None if final else slot + 1
+        total = inside(slot, out, False, None if final else STEPS - 2 - k, not final)
+        finish(slot, out, False, total, not final)
         if k == 1:
             drain(cost_lon, lon_others, lon_send, lon_recv)
             cost_lat[la] = jnp.sum(cost_lon[...], axis=0)
@@ -279,6 +316,7 @@
     n_obs = obs_cell.shape[-1]
     flat = (levels * rows, cols)
     f32 = jnp.float32
+    fold = levels * 2 * rows // cols
     vmem = pl.BlockSpec(memory_space=pltpu.VMEM)
     dma = pltpu.SemaphoreType.DMA
     gradient, cost = pl.pallas_call(
@@ -309,10 +347,10 @@
             pltpu.VMEM((levels, cols), f32),
             pltpu.VMEM((levels, cols), f32),
             pltpu.VMEM((2 * STEPS, 2, levels, cols), f32),
-            pltpu.VMEM((2 * STEPS, 2, levels, cols), f32),
-            pltpu.VMEM((2 * STEPS, levels, cols), f32),
-            pltpu.VMEM((levels, cols), f32),
-            pltpu.VMEM((levels, cols), f32),
+            pltpu.VMEM((2 * STEPS, 2, fold, cols), f32),
+            pltpu.VMEM((2 * STEPS, fold, cols), f32),
+            pltpu.VMEM((fold, cols), f32),
+            pltpu.VMEM((fold, cols), f32),
             pltpu.VMEM((n_lon, 8, 128), f32),
             pltpu.VMEM((n_lat, 8, 128), f32),
             dma((2 * STEPS, 4)),
@@ -326,7 +364,7 @@
             dma((10,)),
         ],
         compiler_params=pltpu.CompilerParams(
-            collective_id=0, has_side_effects=True, vmem_limit_bytes=48 * 1024 * 1024
+            collective_id=0, has_side_effects=True, vmem_limit_bytes=62 * 1024 * 1024
         ),
         cost_estimate=pl.CostEstimate(
             flops=8 * 14 * levels * rows * cols, bytes_accessed=24 * levels * rows * cols, transcendentals=0

time: 58.8 us -> 44.9 us (0.76)
  Pallas kernels: 49.3 us -> 40.5 us
  local copies, waits for them, and re-layouts: 6.7 us -> 1.87 us
    pallas_call x1, Pallas kernels: 49.3 us -> 40.5 us  [on_device(): pl.pallas_call(functools.partial(window, n_lat, n_lon, levels, rows, cols...]
    unnamed x21 -> x1, local copies, waits for them, and re-layouts: 6.7 us -> 1.87 us
where the time goes in v2:
time: 44.9 us; the launch traced here: 44.7 us
  Pallas kernels  40.5 us (90%)
  between operations  2.34 us (5%)
  local copies, waits for them, and re-layouts  1.87 us (4%)
    pallas_call x1, Pallas kernels, on_device(): pl.pallas_call(functools.partial(window, n_lat, n_lon, levels, rows, cols...  40.5 us
    unnamed x1, local copies, waits for them, and re-layouts  1.87 us

profile of v2, /device:TPU:0, one launch (start us, length us, event | category | flops | bytes accessed | tf_op | source)
XLA Modules:
  0.0 44.7 jit_solution(3744979877378014551)
XLA Ops:
  0.6 40.5 %shard_map.113 = (f32[1024,128]{1,0:T(8,128)}, f32[1,1]{1,0:T(1,128)}) custom-call(f32[1024,128]{1,0:T(8,128)} %bitcast.12, f32[1024,128]{1,0:T(8,128)} %bitcast.13, f32[1024,128]{1,0:T(8,128)} %bitcast.14, s32[1024,128]{1,0:T(8,128)} %bitcast.15, s32[1024,128]{1,0:T(8,128)} %bitcast.16, f32[63]{0:T(128)} %refs_5_.1, s32[4,256]{1,0:T(4,128)} %bitcast.17, ...), custom_call_target="tpu_custom_call" | custom-call | flops 14680064 | bytes 3145728 | tf_op jit(solution)/shard_map/pallas_call | solution.py:322
  41.1 1.9 %copy.14 = f32[64,16,128]{2,1,0:T(8,128)} copy(f32[64,16,128]{2,1,0:T(8,128)} %bitcast.11) | data formatting | bytes 1048576

commit v3 on v2

--- a/solution.py
+++ b/solution.py
@@ -175,7 +175,7 @@
             return grad_ref[pl.ds(row, levels, stride=rows), :]
         return field[out, row]
 
-    def inside(t, out, forward, extra, send):
+    def inside(t, out, forward, extra):
         cw, ce, cs, cn = coefs(forward)
         total = jnp.zeros((fold, cols), jnp.float32)
         for row in range(rows):
@@ -192,7 +192,7 @@
             if extra is not None:
                 new = new + source[extra, row * levels : (row + 1) * levels, :]
             put(out, row, new)
-            if send and 0 < row < rows - 1:
+            if out is not None and 0 < row < rows - 1:
                 total = pack(total, new, row)
         return total
 
@@ -215,10 +215,10 @@
         for row in range(1, rows - 1):
             put(out, row, get(out, row) + jnp.where(rim, unpack(gain, row), 0.0))
 
-    def observe(k, slot):
+    def observe(k, slot, final):
         n_obs = cell_ref.shape[1]
-        cell = cell_ref[k : k + 1, :]
-        place = (cell // cols) * levels + level_ref[k : k + 1, :]
+        cell = cell_ref[pl.ds(k, 1), :]
+        place = (cell // cols) * levels + level_ref[pl.ds(k, 1), :]
         col = lax.rem(cell, cols)
         cols_hot = lax.broadcasted_iota(jnp.int32, (cols, n_obs), 0) == col
         pick = jnp.where(cols_hot, 1.0, 0.0).astype(jnp.bfloat16)
@@ -234,8 +234,8 @@
             )
             values = jnp.where(spots == place - row * levels, values, 0.0)
             found = found + jnp.sum(values.reshape(group // 8, 8, n_obs), axis=0)
-        innovation = jnp.sum(found, axis=0, keepdims=True) - value_ref[k : k + 1, :]
-        weighted = weight_ref[k : k + 1, :] * innovation
+        innovation = jnp.sum(found, axis=0, keepdims=True) - value_ref[pl.ds(k, 1), :]
+        weighted = weight_ref[pl.ds(k, 1), :] * innovation
         share = jnp.concatenate(halves(jnp.where(cols_hot, weighted, 0.0)), 0)
 
         for row in range(0, rows, 4):
@@ -244,30 +244,30 @@
                 hot, share, (((1,), (1,)), ((), ())), preferred_element_type=jnp.float32
             )
             value = both[:, :cols] + both[:, cols:]
-            if k == STEPS - 1:
-                field[STEPS, row : row + 4] = value.reshape(4, levels, cols)
+            if final:
+                field[STEPS + 1, row : row + 4] = value.reshape(4, levels, cols)
             else:
                 source[k, row * levels : row * levels + group, :] = value
-        return 0.5 * jnp.sum(weighted * innovation)
-
-    cost = jnp.zeros((), jnp.float32)
-    total = inside(0, 1, True, None, True)
-    for k in range(STEPS):
-        final = k == STEPS - 1
-        slot = 2 * STEPS if final else k + 1
-        finish(k, slot, True, total, not final)
-        if not final:
-            ahead = k + 1 == STEPS - 1
-            total = inside(k + 1, 2 * STEPS if ahead else k + 2, True, None, not ahead)
-        cost = cost + observe(k, slot)
-
-    for copy in row_copies(STEPS):
+        return 0.5 * jnp.sum(weighted * innovation, axis=1, keepdims=True)
+
+    cost = jnp.zeros((1, 1), jnp.float32)
+    def ahead(k, carry):
+        total, cost = carry
+        finish(k, k + 1, True, total, True)
+        total = inside(k + 1, k + 2, True, None)
+        return total, cost + observe(k, k + 1, False)
+
+    total, cost = lax.fori_loop(0, STEPS - 1, ahead, (inside(0, 1, True, None), cost))
+    finish(STEPS - 1, STEPS, True, total, False)
+    cost = cost + observe(STEPS - 1, STEPS, True)
+
+    for copy in row_copies(STEPS + 1):
         copy.start()
     total = jnp.zeros((fold, cols), jnp.float32)
     for row in range(rows):
-        total = pack(total, field[STEPS, row], row)
-    packed[STEPS] = total
-    for copy in col_copies(STEPS):
+        total = pack(total, field[STEPS + 1, row], row)
+    packed[STEPS + 1] = total
+    for copy in col_copies(STEPS + 1):
         copy.start()
 
     def spread(mine, board, others, send, recv):
@@ -282,27 +282,28 @@
             copy.wait_send()
             copy.wait_recv()
 
-    cost_lon[lo] = jnp.full((8, 128), cost, jnp.float32)
+    cost_lon[lo] = jnp.broadcast_to(cost, (8, 128))
     for copy in spread(lo, cost_lon, lon_others, lon_send, lon_recv):
         copy.start()
 
-    for k in range(STEPS):
-        final = k == STEPS - 1
-        slot = STEPS + k
-        out = None if final else slot + 1
-        total = inside(slot, out, False, None if final else STEPS - 2 - k, not final)
-        finish(slot, out, False, total, not final)
-        if k == 1:
-            drain(cost_lon, lon_others, lon_send, lon_recv)
-            cost_lat[la] = jnp.sum(cost_lon[...], axis=0)
-            for copy in spread(la, cost_lat, lat_others, lat_send, lat_recv):
-                copy.start()
+    def back(k, carry):
+        slot = STEPS + 1 + k
+        total = inside(slot, slot + 1, False, STEPS - 2 - k)
+        finish(slot, slot + 1, False, total, True)
+        return carry
+
+    lax.fori_loop(0, STEPS - 1, back, 0)
+    drain(cost_lon, lon_others, lon_send, lon_recv)
+    cost_lat[la] = jnp.sum(cost_lon[...], axis=0)
+    for copy in spread(la, cost_lat, lat_others, lat_send, lat_recv):
+        copy.start()
+    finish(2 * STEPS, None, False, inside(2 * STEPS, None, False, None), False)
     drain(cost_lat, lat_others, lat_send, lat_recv)
     cost_ref[0, 0] = jnp.sum(cost_lat[...], axis=0)[0, 0]
 
     for copy in face_copies:
         copy.wait_send()
-    for t in range(2 * STEPS):
+    for t in [*range(STEPS), *range(STEPS + 1, 2 * STEPS + 1)]:
         for copy in row_copies(t) + col_copies(t):
             copy.wait_send()
 
@@ -346,15 +347,15 @@
             pltpu.VMEM((rows + 1, levels, cols), f32),
             pltpu.VMEM((levels, cols), f32),
             pltpu.VMEM((levels, cols), f32),
-            pltpu.VMEM((2 * STEPS, 2, levels, cols), f32),
-            pltpu.VMEM((2 * STEPS, 2, fold, cols), f32),
-            pltpu.VMEM((2 * STEPS, fold, cols), f32),
+            pltpu.VMEM((2 * STEPS + 1, 2, levels, cols), f32),
+            pltpu.VMEM((2 * STEPS + 1, 2, fold, cols), f32),
+            pltpu.VMEM((2 * STEPS + 1, fold, cols), f32),
             pltpu.VMEM((fold, cols), f32),
             pltpu.VMEM((fold, cols), f32),
             pltpu.VMEM((n_lon, 8, 128), f32),
             pltpu.VMEM((n_lat, 8, 128), f32),
-            dma((2 * STEPS, 4)),
-            dma((2 * STEPS, 4)),
+            dma((2 * STEPS + 1, 4)),
+            dma((2 * STEPS + 1, 4)),
             dma((3,)),
             dma((3,)),
             dma((n_lon - 1,)),
@@ -364,7 +365,7 @@
             dma((10,)),
         ],
         compiler_params=pltpu.CompilerParams(
-            collective_id=0, has_side_effects=True, vmem_limit_bytes=62 * 1024 * 1024
+            collective_id=0, has_side_effects=True, vmem_limit_bytes=54350 * 1024
         ),
         cost_estimate=pl.CostEstimate(
             flops=8 * 14 * levels * rows * cols, bytes_accessed=24 * levels * rows * cols, transcendentals=0

time: 44.9 us -> 44.3 us (0.987)
    unnamed x1 -> x11, local copies, waits for them, and re-layouts: 1.87 us -> 1.49 us
where the time goes in v3:
time: 44.3 us; the launch traced here: 44.1 us
  Pallas kernels  40.2 us (91%)
  between operations  2.37 us (5%)
  local copies, waits for them, and re-layouts  1.49 us (3%)
    pallas_call x1, Pallas kernels, on_device(): pl.pallas_call(functools.partial(window, n_lat, n_lon, levels, rows, cols...  40.2 us
    unnamed x11, local copies, waits for them, and re-layouts  1.49 us

profile of v3, /device:TPU:0, one launch (start us, length us, event | category | flops | bytes accessed | tf_op | source)
XLA Modules:
  0.0 44.1 jit_solution(12716801510886516427)
XLA Ops:
  0.6 0.0 copy-start.3
  0.6 0.0 copy-start.2
  0.7 0.0 copy-start.1
  0.7 0.0 copy-start
  0.7 0.0 copy-start.4
  0.7 0.6 %copy-done.3 = f32[1,1,4,256]{3,2,1,0:T(4,128)S(1)} copy-done((f32[1,1,4,256]{3,2,1,0:T(4,128)S(1)}, f32[1,1,4,256]{3,2,1,0:T(4,128)}, u32[]{:S(2)}) %copy-start.3) | copy-done | bytes 4120
  1.3 0.0 copy-done.2
  1.3 0.0 copy-done.1
  1.4 0.0 copy-done
  1.4 0.0 copy-done.4
  1.4 40.2 %shard_map.113 = (f32[1024,128]{1,0:T(8,128)S(1)}, f32[1,1]{1,0:T(1,128)}) custom-call(f32[1024,128]{1,0:T(8,128)} %bitcast.16, f32[1024,128]{1,0:T(8,128)} %bitcast.17, f32[1024,128]{1,0:T(8,128)} %bitcast.18, s32[1024,128]{1,0:T(8,128)} %bitcast.19, s32[1024,128]{1,0:T(8,128)} %bitcast.20, f32[63]{0:T(128)S(1)} %copy-done.4, s32[4,256]{1,0:T(4,128)S(1)} %bitcast.12, ...), custom_call_target="tpu_custom_call" | custom-call | flops 14680064 | bytes 3145728 | tf_op jit(solution)/shard_map/pallas_call | solution.py:323
  41.6 0.8 %copy.14 = f32[64,16,128]{2,1,0:T(8,128)} copy(f32[64,16,128]{2,1,0:T(8,128)S(1)} %bitcast.11) | data formatting | bytes 1048576
Async XLA Ops:
  0.6 0.7 %copy-start.3 = (f32[1,1,4,256]{3,2,1,0:T(4,128)S(1)}, f32[1,1,4,256]{3,2,1,0:T(4,128)}, u32[]{:S(2)}) copy-start(f32[1,1,4,256]{3,2,1,0:T(4,128)} %param.19) | copy-start | bytes 12292
  0.6 0.7 %copy-start.2 = (f32[1,1,4,256]{3,2,1,0:T(4,128)S(1)}, f32[1,1,4,256]{3,2,1,0:T(4,128)}, u32[]{:S(2)}) copy-start(f32[1,1,4,256]{3,2,1,0:T(4,128)} %param.18) | copy-start | bytes 12292
  0.7 0.7 %copy-start.1 = (s32[1,1,4,256]{3,2,1,0:T(4,128)S(1)}, s32[1,1,4,256]{3,2,1,0:T(4,128)}, u32[]{:S(2)}) copy-start(s32[1,1,4,256]{3,2,1,0:T(4,128)} %param.17) | copy-start | bytes 12292
  0.7 0.7 %copy-start = (s32[1,1,4,256]{3,2,1,0:T(4,128)S(1)}, s32[1,1,4,256]{3,2,1,0:T(4,128)}, u32[]{:S(2)}) copy-start(s32[1,1,4,256]{3,2,1,0:T(4,128)} %param.16) | copy-start | bytes 12292
  0.7 0.7 %copy-start.4 = (f32[63]{0:T(128)S(1)}, f32[63]{0:T(128)}, u32[]{:S(2)}) copy-start(f32[63]{0:T(128)} %refs_5_.1) | copy-start | bytes 760
